TPU v7x, 128 devices: a whole 4x4x4 slice. The times are simulated.
128 devices in a mesh: grp: 16 (over x, y), rep: 8 (over z, core).
Axes of the slice: x: 4, y: 4, z: 4, core: 2. Of those that a mesh axis runs over, the one named last changes fastest.
Arguments:
- tokens: bfloat16 [4096, 4096], P(('rep', 'grp')), parts along dimension 0, may hold values from -6 to 6
- queries: bfloat16 [4096, 4096], P(('rep', 'grp')), parts along dimension 0, may hold values from -16 to 16
- fresh_kv: bfloat16 [4096, 1024], P(('rep', 'grp')), parts along dimension 0, may hold values from -16 to 16
- old_cache: bfloat16 [4096, 32, 1024], P(('rep', 'grp')), parts along dimension 0, may hold values from -16 to 16
- old_slot: int32 [4096], P(('rep', 'grp')), parts along dimension 0, may hold values from 0 to 31, as said below
- new_owner: int32 [4096, 1], P(('rep', 'grp')), parts along dimension 0, may hold values from 0 to 15; in each aligned block of 32 rows (0 to 31, 32 to 63, ...) at most 4 rows name the same one
- lengths: int32 [4096], P(('rep', 'grp')), parts along dimension 0, may hold values from 1 to 31
- norm_gain: bfloat16 [32768], P('rep'), parts along dimension 0, may hold values from 0.099609375 to 1.8984375
- gate_weight: bfloat16 [32768, 14336], P('rep', 'grp'), parts along dimension 0, may hold values from -0.09375 to 0.09375
- up_weight: bfloat16 [32768, 14336], P('rep', 'grp'), parts along dimension 0, may hold values from -0.09375 to 0.09375
- down_weight: bfloat16 [114688, 4096], P(('rep', 'grp')), parts along dimension 0, may hold values from -0.046875 to 0.046875
Outputs:
- layer_out: bfloat16 [4096, 4096], P(('rep', 'grp')), parts along dimension 0
- new_cache: bfloat16 [8192, 32, 1024], P(('rep', 'grp')), parts along dimension 0
There are 8 independent parts, one for each index of `rep`. A program takes and returns all parts, laid end to end along the dimension named above; each array names one. Nothing has to cross between parts.
Inputs may be any that keep to these rules, and one draw needn't show every extreme that they name: `old_slot`: within each aligned block of 32 requests each slot number appears once. `new_owner`: among the rows of one member (aligned blocks of 32) no new member is named more than 4 times, and some new member is named exactly 4 times.
All inputs are finite; a program needn't handle non-finite values.
Results may differ from a plain program's by a relative error of at most 0.017.
Values may be sent and summed in bfloat16 or wider, within the bound.
A program may use at most 128 MiB of HBM per device.

v0:
```python
import jax
import jax.numpy as jnp
from jax import lax
from jax.sharding import PartitionSpec as P

QH = 32
KVH = 4
HD = 128
PER_PEER = 4


def attend(cache_items, query_items, length_items):
    leading = cache_items.shape[:-2]
    cache_len = cache_items.shape[-2]
    width = KVH * HD
    items = cache_items.shape[0]
    key_rows = cache_items[:, :, :width].reshape(items, cache_len, KVH, HD)
    value_rows = cache_items[:, :, width:].reshape(items, cache_len, KVH, HD)
    query_heads = query_items.reshape(items, KVH, QH // KVH, HD)
    scores = jnp.einsum(
        "npkd,nkgd->nkgp", key_rows, query_heads, preferred_element_type=jnp.float32
    )
    scores = scores / jnp.sqrt(jnp.float32(HD))
    valid_mask = jnp.arange(cache_len)[None, :] <= length_items[:, None]
    scores = jnp.where(valid_mask[:, None, None, :], scores, -jnp.inf)
    row_max = jnp.max(scores, axis=-1, keepdims=True)
    expd = jnp.exp(scores - row_max)
    row_total = jnp.sum(expd, axis=-1, keepdims=True)
    weights = (expd / row_total).astype(jnp.bfloat16)
    result = jnp.einsum("nkgp,npkd->nkgd", weights, value_rows, preferred_element_type=jnp.float32)
    return result.reshape(leading + (QH * HD,)).astype(jnp.bfloat16)


def per_device(
    tokens,
    queries,
    fresh_kv,
    old_cache,
    old_slot,
    new_owner,
    lengths,
    norm_gain,
    gate_weight,
    up_weight,
    down_weight,
):
    groups = lax.axis_size("grp")
    local_rows = tokens.shape[0]
    cache_len = old_cache.shape[1]
    kv_width = old_cache.shape[2]
    target = new_owner[:, 0]
    onehot = (target[:, None] == jnp.arange(groups, dtype=jnp.int32)[None, :]).astype(jnp.int32)
    rank_in = jnp.sum((jnp.cumsum(onehot, axis=0) - onehot) * onehot, axis=1)
    flat_slot = target * PER_PEER + rank_in
    slot_table = (
        jnp.full((groups * PER_PEER,), local_rows, jnp.int32)
        .at[flat_slot]
        .set(jnp.arange(local_rows, dtype=jnp.int32))
    )
    held_rows = jnp.take(old_cache, old_slot, axis=0)
    positions = jnp.arange(cache_len, dtype=jnp.int32)
    updated = jnp.where(
        positions[None, :, None] == lengths[:, None, None], fresh_kv[:, None, :], held_rows
    )
    padded_cache = jnp.concatenate(
        [updated, jnp.zeros((1, cache_len, kv_width), jnp.bfloat16)], axis=0
    )
    send_cache = jnp.take(padded_cache, slot_table, axis=0).reshape(
        groups, PER_PEER, cache_len, kv_width
    )
    attended = attend(updated, queries, lengths)
    arrived = lax.all_to_all(send_cache, "grp", split_axis=0, concat_axis=0, tiled=True)
    new_cache = arrived.reshape(groups * PER_PEER, cache_len, kv_width)
    residual = tokens.astype(jnp.float32) + attended.astype(jnp.float32)
    meansq = jnp.mean(residual * residual, axis=-1, keepdims=True)
    normed = (residual * lax.rsqrt(meansq + 1e-05) * norm_gain.astype(jnp.float32)).astype(
        jnp.bfloat16
    )
    piece = lax.all_gather(normed, "grp", axis=0, tiled=True)
    gate_pre = jnp.dot(piece, gate_weight, preferred_element_type=jnp.float32)
    up_pre = jnp.dot(piece, up_weight, preferred_element_type=jnp.float32)
    hidden = (jax.nn.silu(gate_pre) * up_pre).astype(jnp.bfloat16)
    ffn_sum = lax.psum_scatter(
        jnp.dot(hidden, down_weight, preferred_element_type=jnp.float32).astype(jnp.bfloat16),
        "grp",
        scatter_dimension=0,
        tiled=True,
    ).astype(jnp.float32)
    layer_out = (residual + ffn_sum).astype(jnp.bfloat16)
    return (layer_out, new_cache)


def solution(mesh):
    placed = (
        P(("rep", "grp"), None),
        P(("rep", "grp"), None),
        P(("rep", "grp"), None),
        P(("rep", "grp"), None, None),
        P(("rep", "grp")),
        P(("rep", "grp"), None),
        P(("rep", "grp")),
        P("rep"),
        P("rep", "grp"),
        P("rep", "grp"),
        P(("rep", "grp"), None),
    )
    return jax.shard_map(
        per_device,
        mesh=mesh,
        in_specs=placed,
        out_specs=(P(("rep", "grp"), None), P(("rep", "grp"), None, None)),
        check_vma=False,
    )
```

profile of v0, /device:TPU:0, one launch (start us, length us, event | category | flops | bytes accessed | tf_op | source)
XLA Modules:
  0.0 227.1 jit_solution(5596128330964320262)
XLA Ops:
  7.2 0.0 copy-start
  7.2 0.0 copy-start.4
  7.2 0.0 all-gather.2.cloned.1.call-start
  7.2 0.8 compare_select_fusion.2
  8.0 0.7 compare_and_fusion.1
  8.7 0.7 iota_compare_fusion.2
  9.4 0.0 copy-done
  9.4 2.0 gather_fusion
  11.4 0.0 copy-done.4
  11.4 0.0 copy-start.3
  11.5 1.9 select_select_fusion
  13.4 0.0 copy-start.1
  13.4 1.3 copy-done.1
  14.7 1.3 slice_bitcast_fusion.1
  16.1 0.0 copy-start.2
  16.1 0.0 copy-start.5
  16.1 0.0 copy-done.3
  16.1 0.7 fusion.3
  16.8 0.4 fusion.16
  17.2 3.1 %fusion.5 = f32[32,4,8,128]{3,2,1,0:T(8,128)S(1)} fusion(bf16[32,4,4,8,128]{4,3,2,1,0:T(8,128)(2,1)} %get-tuple-element.3, f32[32,4,8]{2,1,0:T(4,128)S(1)} %fusion.16, f32[32,4,8,32]{3,2,1,0:T(8,128)S(1)} %fusion.3), kind=kOutput, calls=%fused_computation.14 | convolution fusion | flops 8750111 | bytes 1708032 | tf_op jit(solution)/shard_map/nkgp,npkd->nkgd/dot_general | solution.py:30
  20.3 0.0 copy-done.2
  20.3 0.4 multiply_reduce_fusion
  20.8 0.0 copy-done.5
  20.8 1.0 multiply_convert_fusion.1
  21.8 0.0 all-gather.2.cloned.1.call-update
  21.8 0.0 reduce-scatter.2.cloned.1.call-start
  21.9 54.0 %all-gather.2.cloned.1.call-done = bf16[512,4096]{1,0:T(8,128)(2,1)} async-done(((bf16[32,4096]{1,0:T(8,128)(2,1)}), bf16[512,4096]{1,0:T(8,128)(2,1)}) %all-gather.2.cloned.1.call-update) | async-done | bytes 4194320 | tf_op jit(solution)/shard_map/all_gather | solution.py:79
  75.8 10.1 %fusion.17 = f32[512,896]{1,0:T(8,128)} fusion(bf16[512,4096]{1,0:T(8,128)(2,1)} %all-gather.2.cloned.1.call-done, bf16[4096,896]{1,0:T(8,128)(2,1)} %param.19), kind=kOutput, calls=%fused_computation.46 | convolution fusion | flops 3758096384 | bytes 13369344 | tf_op jit(solution)/shard_map/dot_general | solution.py:80
  85.9 16.5 %convolution_convert_fusion = bf16[512,4096]{1,0:T(8,128)(2,1)} fusion(bf16[896,4096]{1,0:T(8,128)(2,1)} %param.21, f32[512,896]{1,0:T(8,128)} %fusion.17, bf16[512,4096]{1,0:T(8,128)(2,1)} %all-gather.2.cloned.1.call-done, bf16[4096,896]{1,0:T(8,128)(2,1)} %param.20), kind=kOutput, calls=%fused_computation.4 | convolution fusion | flops 7521042432 | bytes 24903680 | tf_op jit(solution)/shard_map/dot_general | solution.py:84
  102.5 0.0 copy-start.6
  102.5 0.0 reduce-scatter.2.cloned.1.call-update
  102.5 3.2 %concatenate.3 = bf16[33,32,1024]{2,1,0:T(8,128)(2,1)} pad(bf16[32,32,1024]{2,1,0:T(8,128)(2,1)} %copy-done.1, bf16[]{:T(256)} %constant.56.clone.1), padding=0_1x0_0x0_0 | pad | bytes 4259842 | tf_op jit(solution)/shard_map/concatenate | solution.py:65
  105.7 0.0 copy-done.6
  105.7 0.1 fusion.11
  105.8 0.1 reduce_window_sum.11
  105.8 0.2 select_reduce_fusion
  106.0 0.7 scatter_custom_fusion
  106.7 0.1 broadcast_in_dim.78
  106.9 4.3 %gather_fusion.1 = bf16[64,32,1024]{2,1,0:T(8,128)(2,1)} fusion(bf16[33,32,1024]{2,1,0:T(8,128)(2,1)} %concatenate.3, s32[1024]{0:T(1024)S(1)} %pad_clamp_fusion), kind=kCustom, calls=%fused_computation.1 | custom fusion | bytes 8388864 | tf_op jit(solution)/shard_map/jit(_take)/gather | solution.py:68
  111.2 2.7 %broadcast_select_fusion = bf16[16,4,32,1024]{3,2,1,0:T(8,128)(2,1)S(1)} fusion(bf16[16,4,32,1024]{3,2,1,0:T(8,128)(2,1)} %bitcast.42, pred[16,4]{1,0:T(8,128)(4,1)S(1)} %broadcast_in_dim.78), kind=kLoop, calls=%fused_computation.5 | loop fusion | flops 2097152 | bytes 8388672 | tf_op jit(solution)/shard_map/jit(_take)/select_n | solution.py:68
  113.9 65.4 %all_to_all.5 = bf16[16,4,32,1024]{3,2,1,0:T(8,128)(2,1)} all-to-all(bf16[16,4,32,1024]{3,2,1,0:T(8,128)(2,1)S(1)} %broadcast_select_fusion), channel_id=1, replica_groups=mesh['grp'=16,'rep'=8] {'grp'}, dimensions={0} | all-to-all | bytes 8388608 | tf_op jit(solution)/shard_map/all_to_all | solution.py:72
  179.3 34.0 %reduce-scatter.2.cloned.1.call-done = bf16[32,4096]{1,0:T(8,128)(2,1)} async-done(((bf16[512,4096]{1,0:T(8,128)(2,1)}), bf16[32,4096]{1,0:T(8,128)(2,1)}) %reduce-scatter.2.cloned.1.call-update) | async-done | bytes 262160 | tf_op jit(solution)/shard_map/reduce_scatter | solution.py:83
  213.3 2.0 add_convert_fusion
  215.3 5.0 %copy.35 = bf16[64,32,1024]{2,1,0:T(8,128)(2,1)} copy(bf16[64,32,1024]{2,1,0:T(8,128)(2,1)} %bitcast.43) | data formatting | bytes 8388608
  (9 shorter events, 0.1 us)
Async XLA Ops:
  7.2 2.3 %copy-start = (bf16[32,32,1024]{2,1,0:T(8,128)(2,1)S(1)}, bf16[32,32,1024]{2,1,0:T(8,128)(2,1)}, u32[]{:S(2)}) copy-start(bf16[32,32,1024]{2,1,0:T(8,128)(2,1)} %param.14) | copy-start | bytes 6291460
  7.2 4.3 %copy-start.4 = (bf16[32,1024]{1,0:T(8,128)(2,1)S(1)}, bf16[32,1024]{1,0:T(8,128)(2,1)}, u32[]{:S(2)}) copy-start(bf16[32,1024]{1,0:T(8,128)(2,1)} %param.13) | copy-start | bytes 196612
  7.2 68.6 %all-gather.2.cloned.1.call-start = ((), (), s32[]{:S(2)}) async-start(), calls=%async_computation.2 | async-start | bytes 4456448 | tf_op jit(solution)/shard_map/all_gather | solution.py:79
  11.4 4.6 %copy-start.3 = (bf16[32,4096]{1,0:T(8,128)(2,1)S(1)}, bf16[32,4096]{1,0:T(8,128)(2,1)}, u32[]{:S(2)}) copy-start(bf16[32,4096]{1,0:T(8,128)(2,1)} %param.12) | copy-start | bytes 786436
  13.4 1.3 copy-start.1
  16.1 4.2 %copy-start.2 = (bf16[32,4096]{1,0:T(8,128)(2,1)S(1)}, bf16[32,4096]{1,0:T(8,128)(2,1)}, u32[]{:S(2)}) copy-start(bf16[32,4096]{1,0:T(8,128)(2,1)} %param.11) | copy-start | bytes 786436
  16.1 4.7 %copy-start.5 = (bf16[4096]{0:T(1024)(128)(2,1)S(1)}, bf16[4096]{0:T(1024)(128)(2,1)}, u32[]{:S(2)}) copy-start(bf16[4096]{0:T(1024)(128)(2,1)} %param.18) | copy-start | bytes 24580
  21.8 191.5 %reduce-scatter.2.cloned.1.call-start = ((), (), s32[]{:S(2)}) async-start(), calls=%async_computation.3 | async-start | bytes 4456448 | tf_op jit(solution)/shard_map/reduce_scatter | solution.py:83
  102.5 3.2 %copy-start.6 = (s32[32,1]{0,1:T(1,128)S(1)}, s32[32,1]{0,1:T(1,128)}, u32[]{:S(2)}) copy-start(s32[32,1]{0,1:T(1,128)} %param.16) | copy-start | bytes 388
Sparse Core Ops, SparseCore 0:
  21.9 53.8 all-gather.1
  102.6 110.6 reduce-scatter.1
where the time goes:
time: 228 us; the launch traced here: 227 us
  waiting for transfers between devices  88 us (39%)
  blocking collectives  65.4 us (29%)
  matrix products  30.4 us (13%)
  local copies, waits for them, and re-layouts  18.1 us (8%)
  between operations  14.2 us (6%)
  other arithmetic  11 us (5%)
    all_to_all x1, blocking collectives, per_device(): lax.all_to_all(send_cache, 'grp', split_axis=0, concat_axis=0, tiled=True)  65.4 us
    all_gather x1, waiting for transfers between devices, per_device(): piece = lax.all_gather(normed, 'grp', axis=0, tiled=True)  54 us
    reduce_scatter x1, waiting for transfers between devices, per_device(): lax.psum_scatter(jnp.dot(hidden, down_weight, preferred_element_type=jnp....  34 us
    dot_general x1, matrix products, per_device(): jnp.dot(hidden, down_weight, preferred_element_type=jnp.float32)  16.5 us
    dot_general x1, matrix products, per_device(): gate_pre = jnp.dot(piece, gate_weight, preferred_element_type=jnp.float32)  10.1 us
    unnamed x17, local copies, waits for them, and re-layouts  7.74 us
  transfers between devices with their start and end apart: 2, of which 2 were waited for; matrix products, arithmetic and copies ran while one was open for 5% of the time, Pallas kernels for 0%

commit v1 on v0

v1 whole, which is shorter than its diff:
```python
import jax
import jax.numpy as jnp
from jax import lax
from jax.experimental import pallas as pl
from jax.experimental.pallas import tpu as pltpu
from jax.sharding import PartitionSpec as P

KVH = 4
HD = 128
PER_PEER = 4
SIDE = 4
HALF = 16
MESH = pl.DeviceIdType.MESH
ANY = pl.BlockSpec(memory_space=pl.ANY)
SMEM = pl.BlockSpec(memory_space=pltpu.SMEM)
VMEM = pl.BlockSpec(memory_space=pltpu.VMEM)
PEERS = (
    (2, 2), (1, 0), (0, 1), (3, 0), (0, 3), (2, 1), (1, 2), (2, 3),
    (3, 2), (2, 0), (0, 2), (1, 1), (3, 3), (1, 3), (3, 1),
)


def pack_kernel(slot_ref, owner_ref, len_ref, fresh_ref, cache_ref, upd_ref, send_ref,
                held, zero, count, place, in_sem, upd_sem, send_sem):
    rows, cache_len = held.shape[0], held.shape[1]
    members = send_ref.shape[0] // PER_PEER
    for r in range(rows):
        pltpu.make_async_copy(cache_ref.at[slot_ref[r]], held.at[r], in_sem.at[r]).start()
    zero[...] = jnp.zeros_like(zero)
    for m in range(members):
        count[m] = 0
    for r in range(rows):
        owner = owner_ref[r, 0]
        rank = count[owner]
        place[r] = owner * PER_PEER + rank
        count[owner] = rank + 1
    for m in range(members):
        for k in range(PER_PEER):
            s = m * PER_PEER + k

            @pl.when(count[m] <= k)
            def _():
                pltpu.make_async_copy(zero, send_ref.at[s], send_sem.at[s]).start()

    position = lax.broadcasted_iota(jnp.int32, (cache_len, held.shape[2]), 0)
    for r in range(rows):
        pltpu.make_async_copy(cache_ref.at[0], held.at[r], in_sem.at[r]).wait()
        new = jnp.broadcast_to(fresh_ref[r : r + 1, :].astype(jnp.float32), position.shape)
        old = held[r].astype(jnp.float32)
        held[r] = jnp.where(position == len_ref[r], new, old).astype(held.dtype)
        s = place[r]
        pltpu.make_async_copy(held.at[r], send_ref.at[s], send_sem.at[s]).start()
        pltpu.make_async_copy(held.at[r], upd_ref.at[r], upd_sem.at[r]).start()
    for r in range(rows):
        pltpu.make_async_copy(held.at[r], upd_ref.at[r], upd_sem.at[r]).wait()
    for s in range(members * PER_PEER):
        pltpu.make_async_copy(zero, send_ref.at[s], send_sem.at[s]).wait()


def pack(old_slot, new_owner, lengths, fresh_kv, old_cache, members):
    rows, cache_len, width = old_cache.shape
    slots = members * PER_PEER
    return pl.pallas_call(
        pack_kernel,
        name="pack",
        out_shape=[
            jax.ShapeDtypeStruct((rows, cache_len, width), jnp.bfloat16),
            jax.ShapeDtypeStruct((slots, cache_len, width), jnp.bfloat16),
        ],
        in_specs=[SMEM, SMEM, SMEM, VMEM, ANY],
        out_specs=[ANY, ANY],
        scratch_shapes=[
            pltpu.VMEM((rows, cache_len, width), jnp.bfloat16),
            pltpu.VMEM((cache_len, width), jnp.bfloat16),
            pltpu.SMEM((members,), jnp.int32),
            pltpu.SMEM((rows,), jnp.int32),
            pltpu.SemaphoreType.DMA((rows,)),
            pltpu.SemaphoreType.DMA((rows,)),
            pltpu.SemaphoreType.DMA((slots,)),
        ],
        compiler_params=pltpu.CompilerParams(vmem_limit_bytes=16 << 20),
    )(old_slot, new_owner, lengths, fresh_kv, old_cache)


def layer_kernel(len_ref, tok_hbm, q_hbm, gain_hbm, upd_hbm, send_hbm, gate_hbm, up_hbm, down_hbm,
                 newc_ref, out_ref,
                 tok, query, gain, upd, w_in, w_down, full, parts, hidden, residual,
                 r1in, r1own, r1fwd, r2in, r2own, r2fwd,
                 load_sem, w_sem, mig_send, mig_recv, mig_local,
                 ag_send, ag_recv, rs_send, rs_recv):
    rows, width = tok.shape
    mid = width // 2
    left, right = pl.ds(0, mid), pl.ds(mid, mid)
    grp, rep = lax.axis_index("grp"), lax.axis_index("rep")
    x, y = grp // SIDE, grp % SIDE

    def device(px, py):
        return ((px + SIDE) % SIDE * SIDE + (py + SIDE) % SIDE, rep)

    loads = [
        pltpu.make_async_copy(src, dst, load_sem.at[i])
        for i, (src, dst) in enumerate(((upd_hbm, upd), (q_hbm, query), (tok_hbm, tok), (gain_hbm, gain)))
    ]
    for c in loads:
        c.start()
    barrier = pltpu.get_barrier_semaphore()
    for dx, dy in PEERS:
        pl.semaphore_signal(barrier, inc=1, device_id=device(x + dx, y + dy), device_id_type=MESH)
    pl.semaphore_wait(barrier, len(PEERS))

    def migrate(i, k):
        dx, dy = PEERS[i]
        target = device(x + dx, y + dy)
        return pltpu.make_async_remote_copy(
            src_ref=send_hbm.at[target[0] * PER_PEER + k],
            dst_ref=newc_ref.at[grp * PER_PEER + k],
            send_sem=mig_send.at[i, k],
            recv_sem=mig_recv.at[i, k],
            device_id=target,
            device_id_type=MESH,
        )

    def migrate_round(k):
        for i in range(len(PEERS)):
            migrate(i, k).start()

    own_slots = pl.ds(grp * PER_PEER, PER_PEER)
    stay = pltpu.make_async_copy(send_hbm.at[own_slots], newc_ref.at[own_slots], mig_local)
    migrate_round(0)
    stay.start()

    tiles = w_in.shape[0]
    w_copies = []
    for j in range(tiles):
        cols = pl.ds(j * HD, HD)
        w_copies.append(pltpu.make_async_copy(gate_hbm.at[:, cols], w_in.at[j, :, pl.ds(0, HD)], w_sem.at[2 * j]))
        w_copies.append(pltpu.make_async_copy(up_hbm.at[:, cols], w_in.at[j, :, pl.ds(HD, HD)], w_sem.at[2 * j + 1]))
    w_copies.append(pltpu.make_async_copy(down_hbm, w_down, w_sem.at[2 * tiles]))
    for c in loads:
        c.wait()
    for c in w_copies:
        c.start()

    cache_len = upd.shape[1]
    cols_n = rows * cache_len
    row_of = lax.broadcasted_iota(jnp.int32, (rows, cols_n), 0)
    col_of = lax.broadcasted_iota(jnp.int32, (rows, cols_n), 1)
    length = jnp.zeros((8, cols_n), jnp.int32)
    request = lax.broadcasted_iota(jnp.int32, (8, cols_n), 1) // cache_len
    for r in range(rows):
        length = jnp.where(request == r, len_ref[r], length)
    length = jnp.concatenate([length] * (rows // 8), axis=0)
    valid = (col_of // cache_len == row_of) & (col_of % cache_len <= length)
    bias = jnp.where(valid, 0.0, -1e30).astype(jnp.float32)
    heads_per = width // HD // KVH
    bias = jnp.concatenate([bias] * heads_per, axis=0)
    for g in range(KVH):
        keys = upd[:, :, g * HD : (g + 1) * HD].reshape(cols_n, HD)
        values = upd[:, :, (KVH + g) * HD : (KVH + g + 1) * HD].reshape(cols_n, HD)
        heads = [query[:, (g * heads_per + h) * HD : (g * heads_per + h + 1) * HD] for h in range(heads_per)]
        scores = lax.dot_general(
            jnp.concatenate(heads, axis=0), keys, (((1,), (1,)), ((), ())), preferred_element_type=jnp.float32
        )
        scores = scores * (HD**-0.5) + bias
        expd = jnp.exp(scores - jnp.max(scores, axis=1, keepdims=True))
        weights = (expd * (1.0 / jnp.sum(expd, axis=1, keepdims=True))).astype(jnp.bfloat16)
        attended = jnp.dot(weights, values, preferred_element_type=jnp.float32).astype(jnp.bfloat16)
        for h in range(heads_per):
            at = slice((g * heads_per + h) * HD, (g * heads_per + h + 1) * HD)
            residual[:, at] = attended[h * rows : (h + 1) * rows].astype(jnp.float32) + tok[:, at].astype(jnp.float32)
    res = residual[...]
    meansq = jnp.mean(res * res, axis=1, keepdims=True)
    normed = (res * lax.rsqrt(meansq + 1e-05) * gain[...].astype(jnp.float32)).astype(jnp.bfloat16)
    full[x, y] = normed.reshape(2, HALF, width)

    def peer(h, da, db):
        return device(x + da, y + db) if h == 0 else device(x + db, y + da)

    def block(h, da, db):
        px, py = (da, db) if h == 0 else (db, da)
        return ((x + px + SIDE) % SIDE, (y + py + SIDE) % SIDE, h)

    def gather_copy(n, h, da, db, cols, ta, tb):
        ref = full.at[(*block(h, da, db), slice(None), cols)]
        return pltpu.make_async_remote_copy(
            src_ref=ref, dst_ref=ref, send_sem=ag_send.at[h, n], recv_sem=ag_recv.at[h, n],
            device_id=peer(h, ta, tb), device_id_type=MESH,
        )

    everything = pl.ds(0, width)
    sent = []

    def go(copy):
        copy.start()
        sent.append(copy)
        return copy

    ORIGINS = (0, -1, 1, 2)

    def first(h, s):
        return gather_copy(0 if s > 0 else 1, h, 0, 0, everything, s, 0)

    def first_forward(h, s):
        return gather_copy(2 if s > 0 else 3, h, -s, 0, left if s > 0 else right, s, 0)

    def second(h, i, s):
        return gather_copy(4 + 2 * i + (s < 0), h, ORIGINS[i], 0, everything, 0, s)

    def second_forward(h, i, s):
        return gather_copy(12 + 2 * i + (s < 0), h, ORIGINS[i], -s, left if s > 0 else right, 0, s)

    both = (1, -1)
    for h in range(2):
        for s in both:
            go(first(h, s))
    for h in range(2):
        for s in both:
            go(second(h, 0, s))
    for i, s in ((1, 1), (2, -1)):
        for h in range(2):
            first(h, s).wait_recv()
            go(first_forward(h, s))
            for t in both:
                go(second(h, i, t))
    for h in range(2):
        for s in both:
            second(h, 0, s).wait_recv()
            go(second_forward(h, 0, s))
    for h in range(2):
        for s in both:
            first_forward(h, s).wait_recv()
        for t in both:
            go(second(h, 3, t))
    for i in (1, 2, 3):
        for h in range(2):
            for s in both:
                second(h, i, s).wait_recv()
                go(second_forward(h, i, s))
    for i in range(4):
        for h in range(2):
            for s in both:
                second_forward(h, i, s).wait_recv()

    migrate_round(1)
    for c in w_copies:
        c.wait()
    all_rows = SIDE * SIDE * rows

    def up_tile(j, carry):
        pre = jnp.dot(full[...].reshape(all_rows, width), w_in[j], preferred_element_type=jnp.float32)
        gate_pre, up_pre = pre[:, :HD], pre[:, HD:]
        act = gate_pre / (1.0 + jnp.exp(-gate_pre)) * up_pre
        hidden[:, pl.ds(pl.multiple_of(j * HD, HD), HD)] = act.astype(jnp.bfloat16)
        return carry

    lax.fori_loop(0, tiles, up_tile, 0)
    step = 2 * HD

    def down_tile(n, carry):
        cols = pl.ds(pl.multiple_of(n * step, step), step)
        part = jnp.dot(hidden[...], w_down[:, cols], preferred_element_type=jnp.float32)
        parts[:, :, :, :, cols] = part.astype(jnp.bfloat16).reshape(SIDE, SIDE, 2, HALF, step)
        return carry

    lax.fori_loop(0, width // step, down_tile, 0)

    def dest(h, stage, d):
        if stage == 0:
            b = ((y if h == 0 else x) + d + SIDE) % SIDE
            return (slice(None), b, h) if h == 0 else (b, slice(None), h)
        return block(h, d, 0)

    def scatter_copy(n, h, stage, d, cols, s, buf):
        return pltpu.make_async_remote_copy(
            src_ref=parts.at[(*dest(h, stage, d), slice(None), cols)],
            dst_ref=buf.at[h, 0 if s > 0 else 1],
            send_sem=rs_send.at[h, stage, n], recv_sem=rs_recv.at[h, stage, n],
            device_id=peer(h, 0, s) if stage == 0 else peer(h, s, 0), device_id_type=MESH,
        )

    bufs = ((r1in, r1own, r1fwd), (r2in, r2own, r2fwd))

    def far(h, stage, s):
        return scatter_copy(0 if s > 0 else 1, h, stage, 2, left if s > 0 else right, s, bufs[stage][0])

    def near(h, stage, s):
        return scatter_copy(2 if s > 0 else 3, h, stage, s, right if s > 0 else left, s, bufs[stage][1])

    def forward(h, stage, s):
        return scatter_copy(4 if s > 0 else 5, h, stage, s, left if s > 0 else right, s, bufs[stage][2])

    def f32(v):
        return v.astype(jnp.float32)

    for h in range(2):
        for s in both:
            go(far(h, 0, s))
    for h in range(2):
        for s in both:
            go(near(h, 0, s))
    migrate_round(2)
    migrate_round(3)
    for stage in range(2):
        got_far, got_near, got_forward = bufs[stage]
        for h in range(2):
            for s in both:
                far(h, stage, s).wait_recv()
                at = (*dest(h, stage, s), slice(None), left if s > 0 else right)
                parts[at] = (f32(parts[at]) + f32(got_far[h, 0 if s > 0 else 1])).astype(jnp.bfloat16)
                go(forward(h, stage, s))
        for h in range(2):
            sums = []
            for s in both:
                near(h, stage, s).wait_recv()
            for s in both:
                forward(h, stage, s).wait_recv()
                cols = left if s > 0 else right
                at = (*dest(h, stage, 0), slice(None), cols)
                way = 0 if s > 0 else 1
                total = f32(parts[at]) + f32(got_near[h, 1 - way]) + f32(got_forward[h, way])
                if stage == 0:
                    parts[at] = total.astype(jnp.bfloat16)
                else:
                    mine = pl.ds(h * HALF, HALF)
                    tok[mine, cols] = (residual[mine, cols] + total).astype(jnp.bfloat16)
            if stage == 0:
                for s in both:
                    go(far(h, 1, s))
                for s in both:
                    go(near(h, 1, s))
    result = pltpu.make_async_copy(tok, out_ref, load_sem.at[0])
    result.start()

    for copy in sent:
        copy.wait_send()
    stay.wait()
    for k in range(PER_PEER):
        for i in range(len(PEERS)):
            migrate(i, k).wait()
    result.wait()


def layer(lengths, tokens, queries, gain, upd, send, gate_weight, up_weight, down_weight):
    rows, width = tokens.shape
    share = gate_weight.shape[1]
    slots, cache_len, kv_width = send.shape
    mid = width // 2
    bf16 = jnp.bfloat16
    return pl.pallas_call(
        layer_kernel,
        name="layer",
        out_shape=[
            jax.ShapeDtypeStruct((slots, cache_len, kv_width), bf16),
            jax.ShapeDtypeStruct((rows, width), bf16),
        ],
        in_specs=[SMEM] + [ANY] * 8,
        out_specs=[ANY, ANY],
        scratch_shapes=[
            pltpu.VMEM((rows, width), bf16),
            pltpu.VMEM((rows, width), bf16),
            pltpu.VMEM((1, width), bf16),
            pltpu.VMEM(upd.shape, bf16),
            pltpu.VMEM((share // HD, width, 2 * HD), bf16),
            pltpu.VMEM((share, width), bf16),
            pltpu.VMEM((SIDE, SIDE, 2, HALF, width), bf16),
            pltpu.VMEM((SIDE, SIDE, 2, HALF, width), bf16),
            pltpu.VMEM((SIDE * SIDE * rows, share), bf16),
            pltpu.VMEM((rows, width), jnp.float32),
            pltpu.VMEM((2, 2, SIDE, HALF, mid), bf16),
            pltpu.VMEM((2, 2, SIDE, HALF, mid), bf16),
            pltpu.VMEM((2, 2, SIDE, HALF, mid), bf16),
            pltpu.VMEM((2, 2, HALF, mid), bf16),
            pltpu.VMEM((2, 2, HALF, mid), bf16),
            pltpu.VMEM((2, 2, HALF, mid), bf16),
            pltpu.SemaphoreType.DMA((4,)),
            pltpu.SemaphoreType.DMA((2 * (share // HD) + 1,)),
            pltpu.SemaphoreType.DMA((len(PEERS), PER_PEER)),
            pltpu.SemaphoreType.DMA((len(PEERS), PER_PEER)),
            pltpu.SemaphoreType.DMA,
            pltpu.SemaphoreType.DMA((2, 20)),
            pltpu.SemaphoreType.DMA((2, 20)),
            pltpu.SemaphoreType.DMA((2, 2, 6)),
            pltpu.SemaphoreType.DMA((2, 2, 6)),
        ],
        compiler_params=pltpu.CompilerParams(
            collective_id=0, has_side_effects=True, vmem_limit_bytes=60 << 20
        ),
    )(lengths, tokens, queries, gain, upd, send, gate_weight, up_weight, down_weight)


def finish_kernel(newc_ref, out_ref, newc_out, out_out, sems):
    pieces = sems.shape[0] - 1
    size = newc_ref.shape[0] // pieces
    copies = [
        pltpu.make_async_copy(newc_ref.at[pl.ds(i * size, size)], newc_out.at[pl.ds(i * size, size)], sems.at[i])
        for i in range(pieces)
    ]
    copies.append(pltpu.make_async_copy(out_ref, out_out, sems.at[pieces]))
    for c in copies:
        c.start()
    for c in copies:
        c.wait()


def finish(newc, out):
    return pl.pallas_call(
        finish_kernel,
        name="finish",
        out_shape=[jax.ShapeDtypeStruct(newc.shape, newc.dtype), jax.ShapeDtypeStruct(out.shape, out.dtype)],
        in_specs=[ANY, ANY],
        out_specs=[ANY, ANY],
        scratch_shapes=[pltpu.SemaphoreType.DMA((17,))],
    )(newc, out)


def per_device(
    tokens,
    queries,
    fresh_kv,
    old_cache,
    old_slot,
    new_owner,
    lengths,
    norm_gain,
    gate_weight,
    up_weight,
    down_weight,
):
    members = lax.axis_size("grp")
    upd, send = pack(old_slot, new_owner, lengths, fresh_kv, old_cache, members)
    newc, out = layer(
        lengths, tokens, queries, norm_gain.reshape(1, -1), upd, send, gate_weight, up_weight, down_weight
    )
    new_cache, layer_out = finish(newc, out)
    return (layer_out, new_cache)


def solution(mesh):
    placed = (
        P(("rep", "grp"), None),
        P(("rep", "grp"), None),
        P(("rep", "grp"), None),
        P(("rep", "grp"), None, None),
        P(("rep", "grp")),
        P(("rep", "grp"), None),
        P(("rep", "grp")),
        P("rep"),
        P("rep", "grp"),
        P("rep", "grp"),
        P(("rep", "grp"), None),
    )
    return jax.shard_map(
        per_device,
        mesh=mesh,
        in_specs=placed,
        out_specs=(P(("rep", "grp"), None), P(("rep", "grp"), None, None)),
        check_vma=False,
    )
```

time: 228 us -> 270 us (1.18)
  Pallas kernels: 0 us -> 260 us
  waiting for transfers between devices: 88 us -> 0 us
  blocking collectives: 65.4 us -> 0 us
  matrix products: 30.4 us -> 0 us
  between operations: 14.2 us -> 0.66 us
  other arithmetic: 11 us -> 0 us
  local copies, waits for them, and re-layouts: 18.1 us -> 9.12 us
    pallas_call x0 -> x3, Pallas kernels: none -> 260 us  [the longest x1 136 us: finish(): pl.pallas_call(finish_kernel, name='finish', out_shape=[jax.ShapeDtypeStr...]
    all_to_all x1 -> x0, blocking collectives: 65.4 us -> none  [per_device(): lax.all_to_all(send_cache, 'grp', split_axis=0, concat_axis=0, tiled=True)]
    all_gather x1 -> x0, waiting for transfers between devices: 54 us -> none  [per_device(): piece = lax.all_gather(normed, 'grp', axis=0, tiled=True)]
    reduce_scatter x1 -> x0, waiting for transfers between devices: 34 us -> none  [per_device(): lax.psum_scatter(jnp.dot(hidden, down_weight, preferred_element_type=jnp....]
    dot_general x4 -> x0, matrix products: 30.4 us -> none  [the longest x1 16.5 us: per_device(): jnp.dot(hidden, down_weight, preferred_element_type=jnp.float32)]
    gather x2 -> x0, local copies, waits for them, and re-layouts: 6.35 us -> none  [the longest x1 4.35 us: per_device(): jnp.take(padded_cache, slot_table, axis=0)]
    select_n x5 -> x0, other arithmetic: 5.44 us -> none  [the longest x2 2.69 us: per_device(): jnp.take(padded_cache, slot_table, axis=0)]
    concatenate x1 -> x0, local copies, waits for them, and re-layouts: 3.2 us -> none  [per_device(): jnp.concatenate([updated, jnp.zeros((1, cache_len, kv_width), jnp.bfloat1...]
  transfers between devices with their start and end apart: 2 -> 0, of which waited for: 2 -> 0; matrix products, arithmetic and copies ran while one was open for 5% -> 0% of each run, Pallas kernels for 0% -> 0%
where the time goes in v1:
time: 270 us; the launch traced here: 269 us
  Pallas kernels  260 us (96%)
  local copies, waits for them, and re-layouts  9.12 us (3%)
    pallas_call x1, Pallas kernels, finish(): pl.pallas_call(finish_kernel, name='finish', out_shape=[jax.ShapeDtypeStr...  136 us
    pallas_call x1, Pallas kernels, layer(): pl.pallas_call(layer_kernel, name='layer', out_shape=[jax.ShapeDtypeStruc...  109 us
    pallas_call x1, Pallas kernels, pack(): pl.pallas_call(pack_kernel, name='pack', out_shape=[jax.ShapeDtypeStruct(...  14.2 us
    unnamed x13, local copies, waits for them, and re-layouts  7.81 us

profile of v1, /device:TPU:0, one launch (start us, length us, event | category | flops | bytes accessed | tf_op | source)
XLA Modules:
  0.0 269.4 jit_solution(5817537898324377191)
XLA Ops:
  0.6 0.7 copy.13.owner_ref
  1.4 1.3 reshape.7.gain_hbm
  2.7 0.0 copy-start.2
  2.7 1.6 copy-done.2
  4.3 0.0 copy-start.3
  4.3 0.8 copy-done.3
  5.1 0.0 copy-start.4
  5.1 0.7 copy-done.4
  5.8 0.0 copy-start.5
  5.8 0.7 copy-done.5
  6.4 14.2 %pack.1 = (bf16[32,32,1024]{2,1,0:T(8,128)(2,1)S(1)}, bf16[64,32,1024]{2,1,0:T(8,128)(2,1)S(1)}) custom-call(s32[32]{0:T(128)S(1)} %copy-done.5, s32[32,1]{1,0:T(8,128)S(1)} %copy.13.owner_ref, s32[32]{0:T(128)S(1)} %copy-done.4, bf16[32,1024]{1,0:T(8,128)(2,1)S(1)} %copy-done.3, bf16[32,32,1024]{2,1,0:T(8,128)(2,1)S(1)} %copy-done.2), custom_call_target="tpu_custom_call" | custom-call | tf_op jit(solution)/shard_map/pack/pallas_call | solution.py:63
  20.6 0.0 copy-start
  20.6 2.0 copy-done
  22.6 0.0 copy-start.1
  22.6 1.3 copy-done.1
  23.9 109.2 %layer.1 = (bf16[64,32,1024]{2,1,0:T(8,128)(2,1)}, bf16[32,4096]{1,0:T(8,128)(2,1)}) custom-call(s32[32]{0:T(128)} %len_ref.3, bf16[32,4096]{1,0:T(8,128)(2,1)} %tok_hbm.1, bf16[32,4096]{1,0:T(8,128)(2,1)} %q_hbm.1, bf16[1,4096]{1,0:T(2,128)(2,1)} %reshape.7.gain_hbm, bf16[32,32,1024]{2,1,0:T(8,128)(2,1)} %copy-done.1, bf16[64,32,1024]{2,1,0:T(8,128)(2,1)} %copy-done, ...), custom_call_target="tpu_custom_call" | custom-call | tf_op jit(solution)/shard_map/layer/pallas_call | solution.py:349
  133.1 136.3 %finish.1 = (bf16[64,32,1024]{2,1,0:T(8,128)(2,1)}, bf16[32,4096]{1,0:T(8,128)(2,1)}) custom-call(bf16[64,32,1024]{2,1,0:T(8,128)(2,1)} %get-tuple-element.10.newc_ref, bf16[32,4096]{1,0:T(8,128)(2,1)} %get-tuple-element.11.out_ref), custom_call_target="tpu_custom_call" | custom-call | tf_op jit(solution)/shard_map/finish/pallas_call | solution.py:406
Async XLA Ops:
  2.7 1.6 copy-start.2
  4.3 0.8 copy-start.3
  5.1 0.7 copy-start.4
  5.8 0.7 copy-start.5
  20.6 2.0 copy-start
  22.6 1.3 copy-start.1

commit v2 on v1

--- a/solution.py
+++ b/solution.py
@@ -12,79 +12,17 @@
 HALF = 16
 MESH = pl.DeviceIdType.MESH
 ANY = pl.BlockSpec(memory_space=pl.ANY)
-SMEM = pl.BlockSpec(memory_space=pltpu.SMEM)
-VMEM = pl.BlockSpec(memory_space=pltpu.VMEM)
 PEERS = (
     (2, 2), (1, 0), (0, 1), (3, 0), (0, 3), (2, 1), (1, 2), (2, 3),
     (3, 2), (2, 0), (0, 2), (1, 1), (3, 3), (1, 3), (3, 1),
 )
 
 
-def pack_kernel(slot_ref, owner_ref, len_ref, fresh_ref, cache_ref, upd_ref, send_ref,
-                held, zero, count, place, in_sem, upd_sem, send_sem):
-    rows, cache_len = held.shape[0], held.shape[1]
-    members = send_ref.shape[0] // PER_PEER
-    for r in range(rows):
-        pltpu.make_async_copy(cache_ref.at[slot_ref[r]], held.at[r], in_sem.at[r]).start()
-    zero[...] = jnp.zeros_like(zero)
-    for m in range(members):
-        count[m] = 0
-    for r in range(rows):
-        owner = owner_ref[r, 0]
-        rank = count[owner]
-        place[r] = owner * PER_PEER + rank
-        count[owner] = rank + 1
-    for m in range(members):
-        for k in range(PER_PEER):
-            s = m * PER_PEER + k
-
-            @pl.when(count[m] <= k)
-            def _():
-                pltpu.make_async_copy(zero, send_ref.at[s], send_sem.at[s]).start()
-
-    position = lax.broadcasted_iota(jnp.int32, (cache_len, held.shape[2]), 0)
-    for r in range(rows):
-        pltpu.make_async_copy(cache_ref.at[0], held.at[r], in_sem.at[r]).wait()
-        new = jnp.broadcast_to(fresh_ref[r : r + 1, :].astype(jnp.float32), position.shape)
-        old = held[r].astype(jnp.float32)
-        held[r] = jnp.where(position == len_ref[r], new, old).astype(held.dtype)
-        s = place[r]
-        pltpu.make_async_copy(held.at[r], send_ref.at[s], send_sem.at[s]).start()
-        pltpu.make_async_copy(held.at[r], upd_ref.at[r], upd_sem.at[r]).start()
-    for r in range(rows):
-        pltpu.make_async_copy(held.at[r], upd_ref.at[r], upd_sem.at[r]).wait()
-    for s in range(members * PER_PEER):
-        pltpu.make_async_copy(zero, send_ref.at[s], send_sem.at[s]).wait()
-
-
-def pack(old_slot, new_owner, lengths, fresh_kv, old_cache, members):
-    rows, cache_len, width = old_cache.shape
-    slots = members * PER_PEER
-    return pl.pallas_call(
-        pack_kernel,
-        name="pack",
-        out_shape=[
-            jax.ShapeDtypeStruct((rows, cache_len, width), jnp.bfloat16),
-            jax.ShapeDtypeStruct((slots, cache_len, width), jnp.bfloat16),
-        ],
-        in_specs=[SMEM, SMEM, SMEM, VMEM, ANY],
-        out_specs=[ANY, ANY],
-        scratch_shapes=[
-            pltpu.VMEM((rows, cache_len, width), jnp.bfloat16),
-            pltpu.VMEM((cache_len, width), jnp.bfloat16),
-            pltpu.SMEM((members,), jnp.int32),
-            pltpu.SMEM((rows,), jnp.int32),
-            pltpu.SemaphoreType.DMA((rows,)),
-            pltpu.SemaphoreType.DMA((rows,)),
-            pltpu.SemaphoreType.DMA((slots,)),
-        ],
-        compiler_params=pltpu.CompilerParams(vmem_limit_bytes=16 << 20),
-    )(old_slot, new_owner, lengths, fresh_kv, old_cache)
-
-
-def layer_kernel(len_ref, tok_hbm, q_hbm, gain_hbm, upd_hbm, send_hbm, gate_hbm, up_hbm, down_hbm,
+def layer_kernel(tok_hbm, q_hbm, fresh_hbm, cache_hbm, slot_hbm, owner_hbm, len_hbm, gain_hbm,
+                 gate_hbm, up_hbm, down_hbm,
                  newc_ref, out_ref,
-                 tok, query, gain, upd, w_in, w_down, full, parts, hidden, residual,
+                 slot_at, owner_at, len_at, table, table_at,
+                 tok, query, fresh, cache, gain, upd, send, w_in, w_down, full, parts, hidden, residual,
                  r1in, r1own, r1fwd, r2in, r2own, r2fwd,
                  load_sem, w_sem, mig_send, mig_recv, mig_local,
                  ag_send, ag_recv, rs_send, rs_recv):
@@ -97,22 +35,54 @@
     def device(px, py):
         return ((px + SIDE) % SIDE * SIDE + (py + SIDE) % SIDE, rep)
 
-    loads = [
-        pltpu.make_async_copy(src, dst, load_sem.at[i])
-        for i, (src, dst) in enumerate(((upd_hbm, upd), (q_hbm, query), (tok_hbm, tok), (gain_hbm, gain)))
-    ]
+    pairs = (
+        (slot_hbm, slot_at), (owner_hbm, owner_at), (len_hbm, len_at), (cache_hbm, cache), (fresh_hbm, fresh),
+        (q_hbm, query), (tok_hbm, tok), (gain_hbm, gain),
+    )
+    loads = [pltpu.make_async_copy(src, dst, load_sem.at[i]) for i, (src, dst) in enumerate(pairs)]
     for c in loads:
         c.start()
     barrier = pltpu.get_barrier_semaphore()
     for dx, dy in PEERS:
         pl.semaphore_signal(barrier, inc=1, device_id=device(x + dx, y + dy), device_id_type=MESH)
+
+    cache_len, kv_width = cache.shape[1], cache.shape[2]
+    for c in loads[:3]:
+        c.wait()
+    lane = lax.broadcasted_iota(jnp.int32, (rows, 128), 1)
+    sub = lax.broadcasted_iota(jnp.int32, (rows, 128), 0)
+    owner_row = jnp.full((rows, 128), -1, jnp.int32)
+    owner_col = jnp.zeros((rows, 128), jnp.int32)
+    for r in range(rows):
+        owner_row = jnp.where(lane == r, owner_at[r], owner_row)
+        owner_col = jnp.where(sub == r, owner_at[r], owner_col)
+    before = (owner_row == owner_col) & (lane < sub)
+    rank = jnp.sum(before.astype(jnp.int32), axis=1, keepdims=True)
+    fills = (owner_col * PER_PEER + rank == lane).astype(jnp.int32)
+    table[...] = jnp.broadcast_to(rows + jnp.sum(fills * (sub - rows), axis=0, keepdims=True), table.shape)
+    to_smem = pltpu.make_async_copy(table, table_at, load_sem.at[0])
+    to_smem.start()
+
+    for c in loads[3:5]:
+        c.wait()
+    position = lax.broadcasted_iota(jnp.int32, (cache_len, kv_width), 0)
+
+    for r in range(rows):
+        new = jnp.broadcast_to(fresh[r : r + 1, :].astype(jnp.float32), position.shape)
+        old = cache[slot_at[r]].astype(jnp.float32)
+        upd[r] = jnp.where(position == len_at[r], new, old).astype(upd.dtype)
+    upd[rows] = jnp.zeros((cache_len, kv_width), upd.dtype)
+    to_smem.wait()
+    for k in range(PER_PEER):
+        for m in range(SIDE * SIDE):
+            send[m * PER_PEER + k] = upd[table_at[0, m * PER_PEER + k]]
     pl.semaphore_wait(barrier, len(PEERS))
 
     def migrate(i, k):
         dx, dy = PEERS[i]
         target = device(x + dx, y + dy)
         return pltpu.make_async_remote_copy(
-            src_ref=send_hbm.at[target[0] * PER_PEER + k],
+            src_ref=send.at[target[0] * PER_PEER + k],
             dst_ref=newc_ref.at[grp * PER_PEER + k],
             send_sem=mig_send.at[i, k],
             recv_sem=mig_recv.at[i, k],
@@ -125,7 +95,7 @@
             migrate(i, k).start()
 
     own_slots = pl.ds(grp * PER_PEER, PER_PEER)
-    stay = pltpu.make_async_copy(send_hbm.at[own_slots], newc_ref.at[own_slots], mig_local)
+    stay = pltpu.make_async_copy(send.at[own_slots], newc_ref.at[own_slots], mig_local)
     migrate_round(0)
     stay.start()
 
@@ -136,27 +106,26 @@
         w_copies.append(pltpu.make_async_copy(gate_hbm.at[:, cols], w_in.at[j, :, pl.ds(0, HD)], w_sem.at[2 * j]))
         w_copies.append(pltpu.make_async_copy(up_hbm.at[:, cols], w_in.at[j, :, pl.ds(HD, HD)], w_sem.at[2 * j + 1]))
     w_copies.append(pltpu.make_async_copy(down_hbm, w_down, w_sem.at[2 * tiles]))
-    for c in loads:
-        c.wait()
     for c in w_copies:
         c.start()
-
-    cache_len = upd.shape[1]
+    for c in loads[5:]:
+        c.wait()
+
     cols_n = rows * cache_len
     row_of = lax.broadcasted_iota(jnp.int32, (rows, cols_n), 0)
     col_of = lax.broadcasted_iota(jnp.int32, (rows, cols_n), 1)
     length = jnp.zeros((8, cols_n), jnp.int32)
     request = lax.broadcasted_iota(jnp.int32, (8, cols_n), 1) // cache_len
     for r in range(rows):
-        length = jnp.where(request == r, len_ref[r], length)
+        length = jnp.where(request == r, len_at[r], length)
     length = jnp.concatenate([length] * (rows // 8), axis=0)
     valid = (col_of // cache_len == row_of) & (col_of % cache_len <= length)
     bias = jnp.where(valid, 0.0, -1e30).astype(jnp.float32)
     heads_per = width // HD // KVH
     bias = jnp.concatenate([bias] * heads_per, axis=0)
     for g in range(KVH):
-        keys = upd[:, :, g * HD : (g + 1) * HD].reshape(cols_n, HD)
-        values = upd[:, :, (KVH + g) * HD : (KVH + g + 1) * HD].reshape(cols_n, HD)
+        keys = upd[:rows, :, g * HD : (g + 1) * HD].reshape(cols_n, HD)
+        values = upd[:rows, :, (KVH + g) * HD : (KVH + g + 1) * HD].reshape(cols_n, HD)
         heads = [query[:, (g * heads_per + h) * HD : (g * heads_per + h + 1) * HD] for h in range(heads_per)]
         scores = lax.dot_general(
             jnp.concatenate(heads, axis=0), keys, (((1,), (1,)), ((), ())), preferred_element_type=jnp.float32
@@ -170,7 +139,7 @@
             residual[:, at] = attended[h * rows : (h + 1) * rows].astype(jnp.float32) + tok[:, at].astype(jnp.float32)
     res = residual[...]
     meansq = jnp.mean(res * res, axis=1, keepdims=True)
-    normed = (res * lax.rsqrt(meansq + 1e-05) * gain[...].astype(jnp.float32)).astype(jnp.bfloat16)
+    normed = (res * lax.rsqrt(meansq + 1e-05) * gain[...].astype(jnp.float32).reshape(1, width)).astype(jnp.bfloat16)
     full[x, y] = normed.reshape(2, HALF, width)
 
     def peer(h, da, db):
@@ -340,10 +309,11 @@
     result.wait()
 
 
-def layer(lengths, tokens, queries, gain, upd, send, gate_weight, up_weight, down_weight):
+def layer(tokens, queries, fresh_kv, old_cache, old_slot, new_owner, lengths, gain, gate_weight, up_weight, down_weight):
     rows, width = tokens.shape
     share = gate_weight.shape[1]
-    slots, cache_len, kv_width = send.shape
+    _, cache_len, kv_width = old_cache.shape
+    slots = SIDE * SIDE * PER_PEER
     mid = width // 2
     bf16 = jnp.bfloat16
     return pl.pallas_call(
@@ -353,13 +323,21 @@
             jax.ShapeDtypeStruct((slots, cache_len, kv_width), bf16),
             jax.ShapeDtypeStruct((rows, width), bf16),
         ],
-        in_specs=[SMEM] + [ANY] * 8,
+        in_specs=[ANY] * 11,
         out_specs=[ANY, ANY],
         scratch_shapes=[
+            pltpu.SMEM((rows,), jnp.int32),
+            pltpu.SMEM((rows,), jnp.int32),
+            pltpu.SMEM((rows,), jnp.int32),
+            pltpu.VMEM((8, 128), jnp.int32),
+            pltpu.SMEM((8, 128), jnp.int32),
             pltpu.VMEM((rows, width), bf16),
             pltpu.VMEM((rows, width), bf16),
-            pltpu.VMEM((1, width), bf16),
-            pltpu.VMEM(upd.shape, bf16),
+            pltpu.VMEM(fresh_kv.shape, bf16),
+            pltpu.VMEM(old_cache.shape, bf16),
+            pltpu.VMEM((width,), bf16),
+            pltpu.VMEM((rows + 1, cache_len, kv_width), bf16),
+            pltpu.VMEM((slots, cache_len, kv_width), bf16),
             pltpu.VMEM((share // HD, width, 2 * HD), bf16),
             pltpu.VMEM((share, width), bf16),
             pltpu.VMEM((SIDE, SIDE, 2, HALF, width), bf16),
@@ -372,7 +350,7 @@
             pltpu.VMEM((2, 2, HALF, mid), bf16),
             pltpu.VMEM((2, 2, HALF, mid), bf16),
             pltpu.VMEM((2, 2, HALF, mid), bf16),
-            pltpu.SemaphoreType.DMA((4,)),
+            pltpu.SemaphoreType.DMA((8,)),
             pltpu.SemaphoreType.DMA((2 * (share // HD) + 1,)),
             pltpu.SemaphoreType.DMA((len(PEERS), PER_PEER)),
             pltpu.SemaphoreType.DMA((len(PEERS), PER_PEER)),
@@ -385,31 +363,45 @@
         compiler_params=pltpu.CompilerParams(
             collective_id=0, has_side_effects=True, vmem_limit_bytes=60 << 20
         ),
-    )(lengths, tokens, queries, gain, upd, send, gate_weight, up_weight, down_weight)
-
-
-def finish_kernel(newc_ref, out_ref, newc_out, out_out, sems):
-    pieces = sems.shape[0] - 1
-    size = newc_ref.shape[0] // pieces
-    copies = [
-        pltpu.make_async_copy(newc_ref.at[pl.ds(i * size, size)], newc_out.at[pl.ds(i * size, size)], sems.at[i])
-        for i in range(pieces)
-    ]
-    copies.append(pltpu.make_async_copy(out_ref, out_out, sems.at[pieces]))
-    for c in copies:
+    )(
+        tokens, queries, fresh_kv, old_cache, old_slot, new_owner, lengths, gain, gate_weight, up_weight, down_weight
+    )
+
+
+def finish_kernel(newc_ref, out_ref, newc_out, out_out, newc, out, in_sem, out_sem):
+    pieces = in_sem.shape[0] - 1
+    size = newc.shape[0] // pieces
+    ins, outs = [], []
+    for i in range(pieces):
+        at = pl.ds(i * size, size)
+        ins.append(pltpu.make_async_copy(newc_ref.at[at], newc.at[at], in_sem.at[i]))
+        outs.append(pltpu.make_async_copy(newc.at[at], newc_out.at[at], out_sem.at[i]))
+    ins.append(pltpu.make_async_copy(out_ref, out, in_sem.at[pieces]))
+    outs.append(pltpu.make_async_copy(out, out_out, out_sem.at[pieces]))
+    for c in ins:
         c.start()
-    for c in copies:
+    for c, d in zip(ins, outs):
         c.wait()
+        d.start()
+    for d in outs:
+        d.wait()
 
 
 def finish(newc, out):
+    pieces = 8
     return pl.pallas_call(
         finish_kernel,
         name="finish",
         out_shape=[jax.ShapeDtypeStruct(newc.shape, newc.dtype), jax.ShapeDtypeStruct(out.shape, out.dtype)],
         in_specs=[ANY, ANY],
         out_specs=[ANY, ANY],
-        scratch_shapes=[pltpu.SemaphoreType.DMA((17,))],
+        scratch_shapes=[
+            pltpu.VMEM(newc.shape, newc.dtype),
+            pltpu.VMEM(out.shape, out.dtype),
+            pltpu.SemaphoreType.DMA((pieces + 1,)),
+            pltpu.SemaphoreType.DMA((pieces + 1,)),
+        ],
+        compiler_params=pltpu.CompilerParams(vmem_limit_bytes=60 << 20),
     )(newc, out)
 
 
@@ -426,10 +418,9 @@
     up_weight,
     down_weight,
 ):
-    members = lax.axis_size("grp")
-    upd, send = pack(old_slot, new_owner, lengths, fresh_kv, old_cache, members)
     newc, out = layer(
-        lengths, tokens, queries, norm_gain.reshape(1, -1), upd, send, gate_weight, up_weight, down_weight
+        tokens, queries, fresh_kv, old_cache, old_slot, new_owner.reshape(-1), lengths, norm_gain,
+        gate_weight, up_weight, down_weight,
     )
     new_cache, layer_out = finish(newc, out)
     return (layer_out, new_cache)

time: 270 us -> 114 us (0.42)
  Pallas kernels: 260 us -> 113 us
  local copies, waits for them, and re-layouts: 9.12 us -> 0 us
    pallas_call x1, Pallas kernels: 136 us -> 3.78 us  [finish(): pl.pallas_call(finish_kernel, name='finish', out_shape=[jax.ShapeDtypeStr...]
    pallas_call x1 -> x0, Pallas kernels: 14.2 us -> none  [pack(): pl.pallas_call(pack_kernel, name='pack', out_shape=[jax.ShapeDtypeStruct(...]
    unnamed x13 -> x0, local copies, waits for them, and re-layouts: 7.81 us -> none
where the time goes in v2:
time: 114 us
  Pallas kernels  113 us (99%)
    pallas_call x1, Pallas kernels, layer(): pl.pallas_call(layer_kernel, name='layer', out_shape=[jax.ShapeDtypeStruc...  109 us
    pallas_call x1, Pallas kernels, finish(): pl.pallas_call(finish_kernel, name='finish', out_shape=[jax.ShapeDtypeStr...  3.78 us

profile of v2, /device:TPU:0, one launch (start us, length us, event | category | flops | bytes accessed | tf_op | source)
XLA Modules:
  0.0 113.6 jit_solution(8851785390415900754)
XLA Ops:
  0.6 109.1 %layer.1 = (bf16[64,32,1024]{2,1,0:T(8,128)(2,1)}, bf16[32,4096]{1,0:T(8,128)(2,1)}) custom-call(bf16[32,4096]{1,0:T(8,128)(2,1)} %tok_hbm.1, bf16[32,4096]{1,0:T(8,128)(2,1)} %q_hbm.1, bf16[32,1024]{1,0:T(8,128)(2,1)} %fresh_hbm.1, bf16[32,32,1024]{2,1,0:T(8,128)(2,1)} %cache_hbm.1, s32[32]{0:T(128)} %slot_hbm.1, s32[32]{0:T(128)} %bitcast.1, s32[32]{0:T(128)} %len_hbm.1, ...), custom_call_target="tpu_custom_call" | custom-call | tf_op jit(solution)/shard_map/layer/pallas_call | solution.py:319
  109.8 3.8 %finish.1 = (bf16[64,32,1024]{2,1,0:T(8,128)(2,1)}, bf16[32,4096]{1,0:T(8,128)(2,1)}) custom-call(bf16[64,32,1024]{2,1,0:T(8,128)(2,1)} %get-tuple-element.6.newc_ref, bf16[32,4096]{1,0:T(8,128)(2,1)} %get-tuple-element.7.out_ref), custom_call_target="tpu_custom_call" | custom-call | tf_op jit(solution)/shard_map/finish/pallas_call | solution.py:392

commit v3 on v2

--- a/solution.py
+++ b/solution.py
@@ -5,6 +5,8 @@
 from jax.experimental.pallas import tpu as pltpu
 from jax.sharding import PartitionSpec as P
 
+FEED = (20, 0, 0, 0, 0, 0, 0, 0, 20, 6, 6, 4, 4)
+PIECES = 2
 KVH = 4
 HD = 128
 PER_PEER = 4
@@ -78,25 +80,33 @@
             send[m * PER_PEER + k] = upd[table_at[0, m * PER_PEER + k]]
     pl.semaphore_wait(barrier, len(PEERS))
 
-    def migrate(i, k):
+    def slots_copy(amount, send_sem, recv_sem):
+        return pltpu.make_async_remote_copy(
+            src_ref=send.at[pl.ds(0, amount)], dst_ref=newc_ref.at[pl.ds(0, amount)],
+            send_sem=send_sem, recv_sem=recv_sem, device_id=device(x + 1, y), device_id_type=MESH,
+        )
+
+    def migrate(i, k, group):
         dx, dy = PEERS[i]
         target = device(x + dx, y + dy)
         return pltpu.make_async_remote_copy(
             src_ref=send.at[target[0] * PER_PEER + k],
             dst_ref=newc_ref.at[grp * PER_PEER + k],
-            send_sem=mig_send.at[i, k],
-            recv_sem=mig_recv.at[i, k],
+            send_sem=mig_send.at[group],
+            recv_sem=mig_recv.at[group],
             device_id=target,
             device_id_type=MESH,
         )
 
-    def migrate_round(k):
-        for i in range(len(PEERS)):
-            migrate(i, k).start()
+    queue = [(i, k) for k in range(PER_PEER) for i in range(len(PEERS))]
+
+    def feed(point):
+        for _ in range(FEED[point]):
+            migrate(*queue.pop(0), point).start()
 
     own_slots = pl.ds(grp * PER_PEER, PER_PEER)
     stay = pltpu.make_async_copy(send.at[own_slots], newc_ref.at[own_slots], mig_local)
-    migrate_round(0)
+    feed(0)
     stay.start()
 
     tiles = w_in.shape[0]
@@ -152,17 +162,13 @@
     def gather_copy(n, h, da, db, cols, ta, tb):
         ref = full.at[(*block(h, da, db), slice(None), cols)]
         return pltpu.make_async_remote_copy(
-            src_ref=ref, dst_ref=ref, send_sem=ag_send.at[h, n], recv_sem=ag_recv.at[h, n],
+            src_ref=ref, dst_ref=ref, send_sem=ag_send, recv_sem=ag_recv.at[h, n],
             device_id=peer(h, ta, tb), device_id_type=MESH,
         )
 
     everything = pl.ds(0, width)
-    sent = []
-
     def go(copy):
         copy.start()
-        sent.append(copy)
-        return copy
 
     ORIGINS = (0, -1, 1, 2)
 
@@ -185,32 +191,37 @@
     for h in range(2):
         for s in both:
             go(second(h, 0, s))
+    feed(1)
     for i, s in ((1, 1), (2, -1)):
         for h in range(2):
             first(h, s).wait_recv()
             go(first_forward(h, s))
             for t in both:
                 go(second(h, i, t))
+    feed(2)
     for h in range(2):
         for s in both:
             second(h, 0, s).wait_recv()
             go(second_forward(h, 0, s))
+    feed(3)
     for h in range(2):
         for s in both:
             first_forward(h, s).wait_recv()
         for t in both:
             go(second(h, 3, t))
     for i in (1, 2, 3):
+        feed(3 + i)
         for h in range(2):
             for s in both:
                 second(h, i, s).wait_recv()
                 go(second_forward(h, i, s))
+    feed(7)
     for i in range(4):
         for h in range(2):
             for s in both:
                 second_forward(h, i, s).wait_recv()
 
-    migrate_round(1)
+    feed(8)
     for c in w_copies:
         c.wait()
     all_rows = SIDE * SIDE * rows
@@ -224,14 +235,17 @@
 
     lax.fori_loop(0, tiles, up_tile, 0)
     step = 2 * HD
-
-    def down_tile(n, carry):
-        cols = pl.ds(pl.multiple_of(n * step, step), step)
-        part = jnp.dot(hidden[...], w_down[:, cols], preferred_element_type=jnp.float32)
-        parts[:, :, :, :, cols] = part.astype(jnp.bfloat16).reshape(SIDE, SIDE, 2, HALF, step)
-        return carry
-
-    lax.fori_loop(0, width // step, down_tile, 0)
+    piece_width = width // PIECES
+    half_width = piece_width // 2
+
+    def down_piece(p):
+        def down_tile(n, carry):
+            cols = pl.ds(pl.multiple_of(n * step, step), step)
+            part = jnp.dot(hidden[...], w_down[:, cols], preferred_element_type=jnp.float32)
+            parts[:, :, :, :, cols] = part.astype(jnp.bfloat16).reshape(SIDE, SIDE, 2, HALF, step)
+            return carry
+
+        lax.fori_loop(p * piece_width // step, (p + 1) * piece_width // step, down_tile, 0)
 
     def dest(h, stage, d):
         if stage == 0:
@@ -239,73 +253,91 @@
             return (slice(None), b, h) if h == 0 else (b, slice(None), h)
         return block(h, d, 0)
 
-    def scatter_copy(n, h, stage, d, cols, s, buf):
+    def columns(p, side):
+        return pl.ds(p * piece_width + side * half_width, half_width)
+
+    def scatter_copy(n, p, h, stage, d, side, s, buf):
         return pltpu.make_async_remote_copy(
-            src_ref=parts.at[(*dest(h, stage, d), slice(None), cols)],
-            dst_ref=buf.at[h, 0 if s > 0 else 1],
-            send_sem=rs_send.at[h, stage, n], recv_sem=rs_recv.at[h, stage, n],
+            src_ref=parts.at[(*dest(h, stage, d), slice(None), columns(p, side))],
+            dst_ref=buf.at[p, h, 0 if s > 0 else 1],
+            send_sem=rs_send, recv_sem=rs_recv.at[p, h, stage, n],
             device_id=peer(h, 0, s) if stage == 0 else peer(h, s, 0), device_id_type=MESH,
         )
 
     bufs = ((r1in, r1own, r1fwd), (r2in, r2own, r2fwd))
 
-    def far(h, stage, s):
-        return scatter_copy(0 if s > 0 else 1, h, stage, 2, left if s > 0 else right, s, bufs[stage][0])
-
-    def near(h, stage, s):
-        return scatter_copy(2 if s > 0 else 3, h, stage, s, right if s > 0 else left, s, bufs[stage][1])
-
-    def forward(h, stage, s):
-        return scatter_copy(4 if s > 0 else 5, h, stage, s, left if s > 0 else right, s, bufs[stage][2])
+    def far(p, h, stage, s):
+        return scatter_copy(0 if s > 0 else 1, p, h, stage, 2, 0 if s > 0 else 1, s, bufs[stage][0])
+
+    def near(p, h, stage, s):
+        return scatter_copy(2 if s > 0 else 3, p, h, stage, s, 1 if s > 0 else 0, s, bufs[stage][1])
+
+    def forward(p, h, stage, s):
+        return scatter_copy(4 if s > 0 else 5, p, h, stage, s, 0 if s > 0 else 1, s, bufs[stage][2])
 
     def f32(v):
         return v.astype(jnp.float32)
 
-    for h in range(2):
-        for s in both:
-            go(far(h, 0, s))
-    for h in range(2):
-        for s in both:
-            go(near(h, 0, s))
-    migrate_round(2)
-    migrate_round(3)
-    for stage in range(2):
-        got_far, got_near, got_forward = bufs[stage]
-        for h in range(2):
-            for s in both:
-                far(h, stage, s).wait_recv()
-                at = (*dest(h, stage, s), slice(None), left if s > 0 else right)
-                parts[at] = (f32(parts[at]) + f32(got_far[h, 0 if s > 0 else 1])).astype(jnp.bfloat16)
-                go(forward(h, stage, s))
-        for h in range(2):
-            sums = []
-            for s in both:
-                near(h, stage, s).wait_recv()
-            for s in both:
-                forward(h, stage, s).wait_recv()
-                cols = left if s > 0 else right
-                at = (*dest(h, stage, 0), slice(None), cols)
-                way = 0 if s > 0 else 1
-                total = f32(parts[at]) + f32(got_near[h, 1 - way]) + f32(got_forward[h, way])
-                if stage == 0:
-                    parts[at] = total.astype(jnp.bfloat16)
-                else:
-                    mine = pl.ds(h * HALF, HALF)
-                    tok[mine, cols] = (residual[mine, cols] + total).astype(jnp.bfloat16)
+    def send_first(p, h, stage):
+        for s in both:
+            go(far(p, h, stage, s))
+        for s in both:
+            go(near(p, h, stage, s))
+
+    def send_second(p, h, stage):
+        for s in both:
+            far(p, h, stage, s).wait_recv()
+            side = 0 if s > 0 else 1
+            at = (*dest(h, stage, s), slice(None), columns(p, side))
+            parts[at] = (f32(parts[at]) + f32(bufs[stage][0][p, h, side])).astype(jnp.bfloat16)
+            go(forward(p, h, stage, s))
+
+    def sum_own(p, h, stage):
+        for s in both:
+            near(p, h, stage, s).wait_recv()
+        for side, s in enumerate(both):
+            forward(p, h, stage, s).wait_recv()
+            cols = columns(p, side)
+            at = (*dest(h, stage, 0), slice(None), cols)
+            total = f32(parts[at]) + f32(bufs[stage][1][p, h, 1 - side]) + f32(bufs[stage][2][p, h, side])
             if stage == 0:
-                for s in both:
-                    go(far(h, 1, s))
-                for s in both:
-                    go(near(h, 1, s))
+                parts[at] = total.astype(jnp.bfloat16)
+            else:
+                mine = pl.ds(h * HALF, HALF)
+                tok[mine, cols] = (residual[mine, cols] + total).astype(jnp.bfloat16)
+
+    for p in range(PIECES):
+        down_piece(p)
+        for h in range(2):
+            send_first(p, h, 0)
+    feed(9)
+    for p in range(PIECES):
+        for h in range(2):
+            send_second(p, h, 0)
+    feed(10)
+    for p in range(PIECES):
+        for h in range(2):
+            sum_own(p, h, 0)
+            send_first(p, h, 1)
+    feed(11)
+    for p in range(PIECES):
+        for h in range(2):
+            send_second(p, h, 1)
+    feed(12)
+    for p in range(PIECES):
+        for h in range(2):
+            sum_own(p, h, 1)
     result = pltpu.make_async_copy(tok, out_ref, load_sem.at[0])
     result.start()
 
-    for copy in sent:
-        copy.wait_send()
     stay.wait()
-    for k in range(PER_PEER):
-        for i in range(len(PEERS)):
-            migrate(i, k).wait()
+    for point, amount in enumerate(FEED):
+        if amount:
+            together = slots_copy(amount, mig_send.at[point], mig_recv.at[point])
+            together.wait_send()
+            together.wait_recv()
+    slots_copy(len(PEERS) * PER_PEER, ag_send, mig_local).wait_send()
+    slots_copy(len(PEERS) * PER_PEER, rs_send, mig_local).wait_send()
     result.wait()
 
 
@@ -314,7 +346,7 @@
     share = gate_weight.shape[1]
     _, cache_len, kv_width = old_cache.shape
     slots = SIDE * SIDE * PER_PEER
-    mid = width // 2
+    mid = width // PIECES // 2
     bf16 = jnp.bfloat16
     return pl.pallas_call(
         layer_kernel,
@@ -344,21 +376,21 @@
             pltpu.VMEM((SIDE, SIDE, 2, HALF, width), bf16),
             pltpu.VMEM((SIDE * SIDE * rows, share), bf16),
             pltpu.VMEM((rows, width), jnp.float32),
-            pltpu.VMEM((2, 2, SIDE, HALF, mid), bf16),
-            pltpu.VMEM((2, 2, SIDE, HALF, mid), bf16),
-            pltpu.VMEM((2, 2, SIDE, HALF, mid), bf16),
-            pltpu.VMEM((2, 2, HALF, mid), bf16),
-            pltpu.VMEM((2, 2, HALF, mid), bf16),
-            pltpu.VMEM((2, 2, HALF, mid), bf16),
+            pltpu.VMEM((PIECES, 2, 2, SIDE, HALF, mid), bf16),
+            pltpu.VMEM((PIECES, 2, 2, SIDE, HALF, mid), bf16),
+            pltpu.VMEM((PIECES, 2, 2, SIDE, HALF, mid), bf16),
+            pltpu.VMEM((PIECES, 2, 2, HALF, mid), bf16),
+            pltpu.VMEM((PIECES, 2, 2, HALF, mid), bf16),
+            pltpu.VMEM((PIECES, 2, 2, HALF, mid), bf16),
             pltpu.SemaphoreType.DMA((8,)),
             pltpu.SemaphoreType.DMA((2 * (share // HD) + 1,)),
-            pltpu.SemaphoreType.DMA((len(PEERS), PER_PEER)),
-            pltpu.SemaphoreType.DMA((len(PEERS), PER_PEER)),
+            pltpu.SemaphoreType.DMA((len(FEED),)),
+            pltpu.SemaphoreType.DMA((len(FEED),)),
+            pltpu.SemaphoreType.DMA,
             pltpu.SemaphoreType.DMA,
             pltpu.SemaphoreType.DMA((2, 20)),
-            pltpu.SemaphoreType.DMA((2, 20)),
-            pltpu.SemaphoreType.DMA((2, 2, 6)),
-            pltpu.SemaphoreType.DMA((2, 2, 6)),
+            pltpu.SemaphoreType.DMA,
+            pltpu.SemaphoreType.DMA((PIECES, 2, 2, 6)),
         ],
         compiler_params=pltpu.CompilerParams(
             collective_id=0, has_side_effects=True, vmem_limit_bytes=60 << 20

time: 114 us -> 103 us (0.904)
  Pallas kernels: 113 us -> 102 us
    pallas_call x1, Pallas kernels: 109 us -> 98.3 us  [layer(): pl.pallas_call(layer_kernel, name='layer', out_shape=[jax.ShapeDtypeStruc...]
where the time goes in v3:
time: 103 us
  Pallas kernels  102 us (99%)
    pallas_call x1, Pallas kernels, layer(): pl.pallas_call(layer_kernel, name='layer', out_shape=[jax.ShapeDtypeStruc...  98.3 us
    pallas_call x1, Pallas kernels, finish(): pl.pallas_call(finish_kernel, name='finish', out_shape=[jax.ShapeDtypeStr...  3.78 us

profile of v3, /device:TPU:0, one launch (start us, length us, event | category | flops | bytes accessed | tf_op | source)
XLA Modules:
  0.0 102.8 jit_solution(9623468292065076304)
XLA Ops:
  0.6 98.3 %layer.1 = (bf16[64,32,1024]{2,1,0:T(8,128)(2,1)}, bf16[32,4096]{1,0:T(8,128)(2,1)}) custom-call(bf16[32,4096]{1,0:T(8,128)(2,1)} %tok_hbm.1, bf16[32,4096]{1,0:T(8,128)(2,1)} %q_hbm.1, bf16[32,1024]{1,0:T(8,128)(2,1)} %fresh_hbm.1, bf16[32,32,1024]{2,1,0:T(8,128)(2,1)} %cache_hbm.1, s32[32]{0:T(128)} %slot_hbm.1, s32[32]{0:T(128)} %bitcast.1, s32[32]{0:T(128)} %len_hbm.1, ...), custom_call_target="tpu_custom_call" | custom-call | tf_op jit(solution)/shard_map/layer/pallas_call | solution.py:351
  99.0 3.8 %finish.1 = (bf16[64,32,1024]{2,1,0:T(8,128)(2,1)}, bf16[32,4096]{1,0:T(8,128)(2,1)}) custom-call(bf16[64,32,1024]{2,1,0:T(8,128)(2,1)} %get-tuple-element.6.newc_ref, bf16[32,4096]{1,0:T(8,128)(2,1)} %get-tuple-element.7.out_ref), custom_call_target="tpu_custom_call" | custom-call | tf_op jit(solution)/shard_map/finish/pallas_call | solution.py:424

commit v4 on v3

--- a/solution.py
+++ b/solution.py
@@ -5,7 +5,7 @@
 from jax.experimental.pallas import tpu as pltpu
 from jax.sharding import PartitionSpec as P
 
-FEED = (20, 0, 0, 0, 0, 0, 0, 0, 20, 6, 6, 4, 4)
+FEED = (20, 0, 0, 0, 0, 0, 0, 3, 20, 6, 4, 4, 3)
 PIECES = 2
 KVH = 4
 HD = 128
@@ -352,8 +352,8 @@
         layer_kernel,
         name="layer",
         out_shape=[
-            jax.ShapeDtypeStruct((slots, cache_len, kv_width), bf16),
-            jax.ShapeDtypeStruct((rows, width), bf16),
+            pltpu.VMEM((slots, cache_len, kv_width), bf16),
+            pltpu.VMEM((rows, width), bf16),
         ],
         in_specs=[ANY] * 11,
         out_specs=[ANY, ANY],
@@ -393,47 +393,33 @@
             pltpu.SemaphoreType.DMA((PIECES, 2, 2, 6)),
         ],
         compiler_params=pltpu.CompilerParams(
-            collective_id=0, has_side_effects=True, vmem_limit_bytes=60 << 20
+            collective_id=0, has_side_effects=True, vmem_limit_bytes=58 << 20
         ),
     )(
         tokens, queries, fresh_kv, old_cache, old_slot, new_owner, lengths, gain, gate_weight, up_weight, down_weight
     )
 
 
-def finish_kernel(newc_ref, out_ref, newc_out, out_out, newc, out, in_sem, out_sem):
-    pieces = in_sem.shape[0] - 1
-    size = newc.shape[0] // pieces
-    ins, outs = [], []
-    for i in range(pieces):
-        at = pl.ds(i * size, size)
-        ins.append(pltpu.make_async_copy(newc_ref.at[at], newc.at[at], in_sem.at[i]))
-        outs.append(pltpu.make_async_copy(newc.at[at], newc_out.at[at], out_sem.at[i]))
-    ins.append(pltpu.make_async_copy(out_ref, out, in_sem.at[pieces]))
-    outs.append(pltpu.make_async_copy(out, out_out, out_sem.at[pieces]))
-    for c in ins:
+def finish_kernel(newc_ref, out_ref, newc_out, out_out, sems):
+    copies = (
+        pltpu.make_async_copy(newc_ref, newc_out, sems.at[0]),
+        pltpu.make_async_copy(out_ref, out_out, sems.at[1]),
+    )
+    for c in copies:
         c.start()
-    for c, d in zip(ins, outs):
+    for c in copies:
         c.wait()
-        d.start()
-    for d in outs:
-        d.wait()
 
 
 def finish(newc, out):
-    pieces = 8
     return pl.pallas_call(
         finish_kernel,
         name="finish",
         out_shape=[jax.ShapeDtypeStruct(newc.shape, newc.dtype), jax.ShapeDtypeStruct(out.shape, out.dtype)],
         in_specs=[ANY, ANY],
         out_specs=[ANY, ANY],
-        scratch_shapes=[
-            pltpu.VMEM(newc.shape, newc.dtype),
-            pltpu.VMEM(out.shape, out.dtype),
-            pltpu.SemaphoreType.DMA((pieces + 1,)),
-            pltpu.SemaphoreType.DMA((pieces + 1,)),
-        ],
-        compiler_params=pltpu.CompilerParams(vmem_limit_bytes=60 << 20),
+        scratch_shapes=[pltpu.SemaphoreType.DMA((2,))],
+        compiler_params=pltpu.CompilerParams(vmem_limit_bytes=1 << 20),
     )(newc, out)
 
 

time: 103 us -> 100 us (0.971)
  Pallas kernels: 102 us -> 98.9 us
    pallas_call x1, Pallas kernels: 3.78 us -> 2.1 us  [finish(): pl.pallas_call(finish_kernel, name='finish', out_shape=[jax.ShapeDtypeStr...]
    pallas_call x1, Pallas kernels: 98.3 us -> 96.8 us  [layer(): pl.pallas_call(layer_kernel, name='layer', out_shape=[pltpu.VMEM((slots,...]
where the time goes in v4:
time: 100 us; the launch traced here: 99.5 us
  Pallas kernels  98.9 us (99%)
    pallas_call x1, Pallas kernels, layer(): pl.pallas_call(layer_kernel, name='layer', out_shape=[pltpu.VMEM((slots,...  96.8 us
    pallas_call x1, Pallas kernels, finish(): pl.pallas_call(finish_kernel, name='finish', out_shape=[jax.ShapeDtypeStr...  2.1 us

profile of v4, /device:TPU:0, one launch (start us, length us, event | category | flops | bytes accessed | tf_op | source)
XLA Modules:
  0.0 99.5 jit_solution(10300412278119271317)
XLA Ops:
  0.6 96.8 %layer.1 = (bf16[64,32,1024]{2,1,0:T(8,128)(2,1)S(1)}, bf16[32,4096]{1,0:T(8,128)(2,1)S(1)}) custom-call(bf16[32,4096]{1,0:T(8,128)(2,1)} %tok_hbm.1, bf16[32,4096]{1,0:T(8,128)(2,1)} %q_hbm.1, bf16[32,1024]{1,0:T(8,128)(2,1)} %fresh_hbm.1, bf16[32,32,1024]{2,1,0:T(8,128)(2,1)} %cache_hbm.1, s32[32]{0:T(128)} %slot_hbm.1, s32[32]{0:T(128)} %bitcast.1, ...), custom_call_target="tpu_custom_call" | custom-call | tf_op jit(solution)/shard_map/layer/pallas_call | solution.py:351
  97.4 2.1 %finish.1 = (bf16[64,32,1024]{2,1,0:T(8,128)(2,1)}, bf16[32,4096]{1,0:T(8,128)(2,1)}) custom-call(bf16[64,32,1024]{2,1,0:T(8,128)(2,1)S(1)} %get-tuple-element.6.newc_ref, bf16[32,4096]{1,0:T(8,128)(2,1)S(1)} %get-tuple-element.7.out_ref), custom_call_target="tpu_custom_call" | custom-call | tf_op jit(solution)/shard_map/finish/pallas_call | solution.py:415

commit v5 on v4

--- a/solution.py
+++ b/solution.py
@@ -5,7 +5,7 @@
 from jax.experimental.pallas import tpu as pltpu
 from jax.sharding import PartitionSpec as P
 
-FEED = (20, 0, 0, 0, 0, 0, 0, 3, 20, 6, 4, 4, 3)
+FEED = (20, 0, 0, 0, 0, 0, 0, 3, 20, 0, 8, 6, 3)
 PIECES = 2
 KVH = 4
 HD = 128
@@ -37,6 +37,9 @@
     def device(px, py):
         return ((px + SIDE) % SIDE * SIDE + (py + SIDE) % SIDE, rep)
 
+    barrier = pltpu.get_barrier_semaphore()
+    for dx, dy in PEERS:
+        pl.semaphore_signal(barrier, inc=1, device_id=device(x + dx, y + dy), device_id_type=MESH)
     pairs = (
         (slot_hbm, slot_at), (owner_hbm, owner_at), (len_hbm, len_at), (cache_hbm, cache), (fresh_hbm, fresh),
         (q_hbm, query), (tok_hbm, tok), (gain_hbm, gain),
@@ -44,9 +47,6 @@
     loads = [pltpu.make_async_copy(src, dst, load_sem.at[i]) for i, (src, dst) in enumerate(pairs)]
     for c in loads:
         c.start()
-    barrier = pltpu.get_barrier_semaphore()
-    for dx, dy in PEERS:
-        pl.semaphore_signal(barrier, inc=1, device_id=device(x + dx, y + dy), device_id_type=MESH)
 
     cache_len, kv_width = cache.shape[1], cache.shape[2]
     for c in loads[:3]:

time: 100 us -> 99.5 us (level)
  no operation moved by 1% of the time
where the time goes in v5:
time: 99.5 us; the launch traced here: 99.3 us
  Pallas kernels  98.7 us (99%)
    pallas_call x1, Pallas kernels, layer(): pl.pallas_call(layer_kernel, name='layer', out_shape=[pltpu.VMEM((slots,...  96.6 us
    pallas_call x1, Pallas kernels, finish(): pl.pallas_call(finish_kernel, name='finish', out_shape=[jax.ShapeDtypeStr...  2.1 us

profile of v5, /device:TPU:0, one launch (start us, length us, event | category | flops | bytes accessed | tf_op | source)
XLA Modules:
  0.0 99.3 jit_solution(5702152888060674720)
XLA Ops:
  0.6 96.6 %layer.1 = (bf16[64,32,1024]{2,1,0:T(8,128)(2,1)S(1)}, bf16[32,4096]{1,0:T(8,128)(2,1)S(1)}) custom-call(bf16[32,4096]{1,0:T(8,128)(2,1)} %tok_hbm.1, bf16[32,4096]{1,0:T(8,128)(2,1)} %q_hbm.1, bf16[32,1024]{1,0:T(8,128)(2,1)} %fresh_hbm.1, bf16[32,32,1024]{2,1,0:T(8,128)(2,1)} %cache_hbm.1, s32[32]{0:T(128)} %slot_hbm.1, s32[32]{0:T(128)} %bitcast.1, ...), custom_call_target="tpu_custom_call" | custom-call | tf_op jit(solution)/shard_map/layer/pallas_call | solution.py:351
  97.2 2.1 %finish.1 = (bf16[64,32,1024]{2,1,0:T(8,128)(2,1)}, bf16[32,4096]{1,0:T(8,128)(2,1)}) custom-call(bf16[64,32,1024]{2,1,0:T(8,128)(2,1)S(1)} %get-tuple-element.6.newc_ref, bf16[32,4096]{1,0:T(8,128)(2,1)S(1)} %get-tuple-element.7.out_ref), custom_call_target="tpu_custom_call" | custom-call | tf_op jit(solution)/shard_map/finish/pallas_call | solution.py:415

commit v6 on v5

--- a/solution.py
+++ b/solution.py
@@ -75,9 +75,14 @@
         upd[r] = jnp.where(position == len_at[r], new, old).astype(upd.dtype)
     upd[rows] = jnp.zeros((cache_len, kv_width), upd.dtype)
     to_smem.wait()
-    for k in range(PER_PEER):
-        for m in range(SIDE * SIDE):
-            send[m * PER_PEER + k] = upd[table_at[0, m * PER_PEER + k]]
+
+    def fill(rounds):
+        for k in rounds:
+            for m in range(SIDE * SIDE):
+                send[m * PER_PEER + k] = upd[table_at[0, m * PER_PEER + k]]
+
+    at_once = -(-FEED[0] // len(PEERS))
+    fill(range(at_once))
     pl.semaphore_wait(barrier, len(PEERS))
 
     def slots_copy(amount, send_sem, recv_sem):
@@ -107,6 +112,7 @@
     own_slots = pl.ds(grp * PER_PEER, PER_PEER)
     stay = pltpu.make_async_copy(send.at[own_slots], newc_ref.at[own_slots], mig_local)
     feed(0)
+    fill(range(at_once, PER_PEER))
     stay.start()
 
     tiles = w_in.shape[0]

time: 99.5 us -> 99.5 us (level)
  no operation moved by 1% of the time
where the time goes in v6:
time: 99.5 us; the launch traced here: 99.3 us
  Pallas kernels  98.7 us (99%)
    pallas_call x1, Pallas kernels, layer(): pl.pallas_call(layer_kernel, name='layer', out_shape=[pltpu.VMEM((slots,...  96.6 us
    pallas_call x1, Pallas kernels, finish(): pl.pallas_call(finish_kernel, name='finish', out_shape=[jax.ShapeDtypeStr...  2.1 us

profile of v6, /device:TPU:0, one launch (start us, length us, event | category | flops | bytes accessed | tf_op | source)
XLA Modules:
  0.0 99.3 jit_solution(8145488316988532819)
XLA Ops:
  0.6 96.6 %layer.1 = (bf16[64,32,1024]{2,1,0:T(8,128)(2,1)S(1)}, bf16[32,4096]{1,0:T(8,128)(2,1)S(1)}) custom-call(bf16[32,4096]{1,0:T(8,128)(2,1)} %tok_hbm.1, bf16[32,4096]{1,0:T(8,128)(2,1)} %q_hbm.1, bf16[32,1024]{1,0:T(8,128)(2,1)} %fresh_hbm.1, bf16[32,32,1024]{2,1,0:T(8,128)(2,1)} %cache_hbm.1, s32[32]{0:T(128)} %slot_hbm.1, s32[32]{0:T(128)} %bitcast.1, ...), custom_call_target="tpu_custom_call" | custom-call | tf_op jit(solution)/shard_map/layer/pallas_call | solution.py:357
  97.2 2.1 %finish.1 = (bf16[64,32,1024]{2,1,0:T(8,128)(2,1)}, bf16[32,4096]{1,0:T(8,128)(2,1)}) custom-call(bf16[64,32,1024]{2,1,0:T(8,128)(2,1)S(1)} %get-tuple-element.6.newc_ref, bf16[32,4096]{1,0:T(8,128)(2,1)S(1)} %get-tuple-element.7.out_ref), custom_call_target="tpu_custom_call" | custom-call | tf_op jit(solution)/shard_map/finish/pallas_call | solution.py:421
